TPU v7x, 128 devices: a whole 4x4x4 slice. The times are simulated.
128 devices in a mesh: seq: 16 (over y, x), mp: 8 (over z, core).
Axes of the slice: x: 4, y: 4, z: 4, core: 2. Of those that a mesh axis runs over, the one named last changes fastest.
Arguments:
- residual_activations: bfloat16 [16384, 4096], P('seq', 'mp'), may hold values from -6 to 6
- prelayer_gain_vector: bfloat16 [4096], replicated, may hold values from 0.099609375 to 1.8984375
- gating_projection: bfloat16 [4096], replicated, may hold values from -0.25 to 0.25
- asker_projection: bfloat16 [4096, 8192], P(None, 'mp'), may hold values from -0.09375 to 0.09375
- lookup_projection: bfloat16 [4096, 1024], P(None, 'mp'), may hold values from -0.09375 to 0.09375
- content_projection: bfloat16 [4096, 1024], P(None, 'mp'), may hold values from -0.09375 to 0.09375
- final_projection: bfloat16 [8192, 4096], P(None, 'mp'), may hold values from -0.0625 to 0.0625
- logit_sharpness: float32 [64], P('mp'), may hold values from 1 to 64
- selection_table: int32 [16, 256], P('seq'), may hold values from 0 to 1023, as said below
- dispatched_tally_table: int32 [16, 16], replicated, may hold values from 0 to 16, as said below
Outputs:
- blended: bfloat16 [16384, 4096], P('seq', 'mp')
Inputs may be any that keep to these rules, and one draw needn't show every extreme that they name: `dispatched_tally_table`: entry [s, d] counts the routed tokens of source shard s whose compacted place falls to owner d: the compacted sequence lists all routed tokens in sequence order and is dealt in blocks of 8 places, block b to owner b mod 16. Every entry is a multiple of 8, and every column sums to 128. `selection_table`: row s lists in increasing order the distinct local indices of the routed tokens of source shard s, as many as row s of dispatched_tally_table sums to, and zeros after them.
All inputs are finite; a program needn't handle non-finite values.
Results may differ from a plain program's by a relative error of at most 0.0059.
Values may be sent and summed in bfloat16 or wider, within the bound.
No kernel may reach another device: no remote copies, remote signals or barrier semaphores. Data moves between devices by JAX's collectives and lax.ppermute only.
A program may use at most 64 MiB of HBM per device.

v0:
```python
import math
import jax
import jax.numpy as jnp
from jax import lax
from jax.sharding import PartitionSpec as P

HEADS = 64
SHARED_KV_COUNT = 8
PER_HEAD_DIM = 128
SEL = 128


def compact(incoming, prefix, spans, shard, nseq, owned):
    span_ids = jnp.arange(nseq, dtype=jnp.int32) * nseq + shard
    source_of = jnp.sum(
        (prefix[None, :] + spans[None, :] <= span_ids[:, None]).astype(jnp.int32), axis=1
    )
    matches = source_of[:, None] == jnp.arange(nseq, dtype=jnp.int32)[None, :]
    start_of = jnp.sum(jnp.where(matches, prefix[None, :], 0), axis=1)
    half_of = (span_ids - start_of) // nseq
    blocks = incoming.reshape(2 * nseq, incoming.shape[2], incoming.shape[3])
    return blocks[half_of * nseq + source_of].reshape(owned, incoming.shape[3])


def build_return(delta, prefix, spans, shard, nseq, block_rows):
    first = (shard - prefix) % nseq
    counter = jnp.arange(2, dtype=jnp.int32)[:, None] * nseq + first[None, :]
    usable = counter < spans[None, :]
    target = jnp.minimum((prefix[None, :] + counter) // nseq, nseq - 1)
    blocks = delta.reshape(nseq, block_rows, delta.shape[1])[target]
    return jnp.where(usable[:, :, None, None], blocks, jnp.zeros_like(blocks))


def on_device(
    residual_activations,
    prelayer_gain_vector,
    gating_projection,
    asker_projection,
    lookup_projection,
    content_projection,
    final_projection,
    logit_sharpness,
    selection_table,
    dispatched_tally_table,
):
    nseq = lax.axis_size("seq")
    shard = lax.axis_index("seq")
    owned = SEL
    block_rows = owned // nseq
    slots = selection_table.shape[1]
    sent = jnp.sum(dispatched_tally_table, axis=1)
    spans = sent // block_rows
    prefix = jnp.cumsum(spans) - spans
    mine = jnp.arange(nseq, dtype=jnp.int32) == shard
    my_prefix = jnp.sum(jnp.where(mine, prefix, 0))
    my_sent = jnp.sum(jnp.where(mine, sent, 0))
    rotation = my_prefix % nseq
    index_list = selection_table[0]
    live = jnp.arange(slots) < my_sent
    gathered_rows = residual_activations[index_list]
    gathered_rows = jnp.where(live[:, None], gathered_rows, jnp.zeros_like(gathered_rows))
    whole_rows = lax.all_gather(gathered_rows, "mp", axis=1, tiled=True)
    outgoing = jnp.roll(
        whole_rows.reshape(2, nseq, block_rows, whole_rows.shape[1]), rotation, axis=1
    )
    incoming = lax.all_to_all(outgoing, "seq", split_axis=1, concat_axis=1, tiled=True)
    full = compact(incoming, prefix, spans, shard, nseq, owned)
    gate = jax.nn.sigmoid(jnp.dot(full, gating_projection, preferred_element_type=jnp.float32))
    widened = full.astype(jnp.float32)
    inverse = lax.rsqrt(jnp.mean(widened * widened, axis=1, keepdims=True) + 1e-05)
    normed = (widened * inverse * prelayer_gain_vector.astype(jnp.float32)).astype(jnp.bfloat16)
    query = jnp.dot(normed, asker_projection, preferred_element_type=jnp.float32).astype(
        jnp.bfloat16
    )
    keys = jnp.dot(normed, lookup_projection, preferred_element_type=jnp.float32).astype(
        jnp.bfloat16
    )
    values = jnp.dot(normed, content_projection, preferred_element_type=jnp.float32).astype(
        jnp.bfloat16
    )
    paired = jnp.stack([keys, values])
    memory_pair_portion = lookup_projection.shape[1] // PER_HEAD_DIM
    asker_cluster = HEADS // SHARED_KV_COUNT
    query_heads = query.reshape(owned, memory_pair_portion, asker_cluster, PER_HEAD_DIM)
    gating_multipliers = logit_sharpness.reshape(memory_pair_portion, asker_cluster) / math.sqrt(
        PER_HEAD_DIM
    )
    own_slots = jnp.arange(owned, dtype=jnp.int32)
    query_places = (
        own_slots // block_rows * nseq * block_rows + shard * block_rows + own_slots % block_rows
    )
    start_best = jnp.full((memory_pair_portion, asker_cluster, owned), -1e30, jnp.float32)
    piece = lax.all_gather(paired, "seq", axis=1, tiled=True)
    best = start_best
    count = piece.shape[1]
    key_piece = piece[0].reshape(count, memory_pair_portion, PER_HEAD_DIM)
    value_piece = piece[1].reshape(count, memory_pair_portion, PER_HEAD_DIM)
    index_all = jnp.arange(count, dtype=jnp.int32)
    owner = index_all // owned
    position = index_all % owned
    key_places = (
        position // block_rows * nseq * block_rows + owner * block_rows + position % block_rows
    )
    allowed = key_places[None, :] <= query_places[:, None]
    score = jnp.einsum("qngd,knd->ngqk", query_heads, key_piece, preferred_element_type=jnp.float32)
    score = jnp.where(allowed[None, None], score * gating_multipliers[:, :, None, None], -1e30)
    new_best = jnp.maximum(best, jnp.max(score, axis=3))
    weights = jnp.where(allowed[None, None], jnp.exp(score - new_best[..., None]), 0.0)
    totals = jnp.sum(weights, axis=3)
    mixed = jnp.einsum(
        "ngqk,knd->ngqd",
        weights.astype(jnp.bfloat16),
        value_piece,
        preferred_element_type=jnp.float32,
    )
    sums = mixed
    best, totals, sums = (new_best, totals, sums)
    attended = (sums / totals[..., None]).astype(jnp.bfloat16)
    attended = attended.transpose(2, 0, 1, 3).reshape(
        owned, memory_pair_portion * asker_cluster * PER_HEAD_DIM
    )
    projected = jnp.dot(
        lax.all_gather(attended, "mp", axis=1, tiled=True),
        final_projection,
        preferred_element_type=jnp.float32,
    )
    delta = (gate[:, None] * projected).astype(jnp.bfloat16)
    outgoing_back = build_return(delta, prefix, spans, shard, nseq, block_rows)
    coming_back = lax.all_to_all(outgoing_back, "seq", split_axis=1, concat_axis=1, tiled=True)
    restored = jnp.roll(coming_back, -rotation, axis=1).reshape(slots, delta.shape[1])
    restored = jnp.where(live[:, None], restored, jnp.zeros_like(restored))
    updated = (
        residual_activations.astype(jnp.float32).at[index_list].add(restored.astype(jnp.float32))
    )
    return updated.astype(jnp.bfloat16)


def solution(mesh):
    placed = (
        P("seq", "mp"),
        P(),
        P(),
        P(None, "mp"),
        P(None, "mp"),
        P(None, "mp"),
        P(None, "mp"),
        P("mp"),
        P("seq", None),
        P(),
    )
    return jax.shard_map(
        on_device, mesh=mesh, in_specs=placed, out_specs=P("seq", "mp"), check_vma=False
    )
```

profile of v0, /device:TPU:1, one launch (start us, length us, event | category | flops | bytes accessed | tf_op | source)
XLA Modules:
  0.0 201.7 jit_solution(617594323271170253)
XLA Ops:
  6.5 0.9 reduce_sum.69
  9.7 2.6 %gather_fusion = bf16[256,512]{1,0:T(8,128)(2,1)S(1)} fusion(bf16[1024,512]{1,0:T(8,128)(2,1)} %param.10, s32[1024]{0:T(1024)S(1)} %pad_clamp_fusion.2), kind=kCustom, calls=%fused_computation | custom fusion | bytes 525312 | tf_op jit(solution)/shard_map/gather | solution.py:60
  12.3 0.8 broadcast_select_fusion
  15.6 26.6 %all-gather.4.cloned.1.call-done = bf16[256,4096]{1,0:T(8,128)(2,1)} async-done(((bf16[256,512]{1,0:T(8,128)(2,1)}), bf16[256,4096]{1,0:T(8,128)(2,1)}) %all-gather.4.cloned.1.call-update) | async-done | bytes 2097168 | tf_op jit(solution)/shard_map/all_gather | solution.py:62
  42.3 2.4 %fusion.7 = bf16[2,16,8,4096]{3,2,1,0:T(8,128)(2,1)S(1)} fusion(s32[]{:T(128)S(6)} %select_n.208, bf16[2,16,8,4096]{3,2,1,0:T(8,128)(2,1)} %bitcast.124), kind=kLoop, calls=%fused_computation.15 | loop fusion | flops 1048576 | bytes 4194308 | tf_op jit(solution)/shard_map/jit(_roll_dynamic)/concatenate | solution.py:63
  44.6 1.5 copy.48
  46.1 6.6 %all-to-all-start = ((bf16[2,16,8,4096]{3,2,0,1:T(8,128)(2,1)}), bf16[2,16,8,4096]{3,2,0,1:T(8,128)(2,1)S(1)}, u32[]{:S(2)}, u32[]{:S(2)}) async-start(bf16[2,16,8,4096]{3,2,0,1:T(8,128)(2,1)} %copy.48), calls=%async_computation | async-start | bytes 4194304 | tf_op jit(solution)/shard_map/all_to_all | solution.py:66
  53.2 32.2 %all-to-all-done = bf16[2,16,8,4096]{3,2,0,1:T(8,128)(2,1)S(1)} async-done(((bf16[2,16,8,4096]{3,2,0,1:T(8,128)(2,1)}), bf16[2,16,8,4096]{3,2,0,1:T(8,128)(2,1)S(1)}, u32[]{:S(2)}, u32[]{:S(2)}) %all-to-all-start) | async-done | bytes 2097184 | tf_op jit(solution)/shard_map/all_to_all | solution.py:66
  85.4 1.5 copy.38
  86.9 2.2 %gather_fusion.1 = bf16[16,8,4096]{2,1,0:T(8,128)(2,1)S(1)} fusion(bf16[32,8,4096]{2,1,0:T(8,128)(2,1)} %bitcast.123, s32[1024]{0:T(1024)S(1)} %pad_clamp_fusion.1), kind=kCustom, calls=%fused_computation.1 | custom fusion | bytes 2097216 | tf_op jit(solution)/shard_map/gather | solution.py:22
  90.0 1.7 fusion.12
  92.9 4.7 %fusion.8 = bf16[16,8,8,128]{3,2,1,0:T(8,128)(2,1)S(1)} fusion(bf16[4096,1024]{1,0:T(8,128)(2,1)} %param.13, bf16[16,8,4096]{2,1,0:T(8,128)(2,1)S(1)} %gather_fusion.1, f32[4096]{0:T(1024)S(1)} %convert_element_type.49, f32[128]{0:T(128)S(1)} %rsqrt.12), kind=kOutput, calls=%fused_computation.20 | convolution fusion | flops 1075970048 | bytes 9716224 | tf_op jit(solution)/shard_map/dot_general | solution.py:72
  97.6 34.0 %all-gather.6.cloned.1.call-done = bf16[2,2048,128]{2,1,0:T(8,128)(2,1)} async-done(((bf16[2,128,128]{2,1,0:T(8,128)(2,1)}), bf16[2,2048,128]{2,1,0:T(8,128)(2,1)}) %all-gather.6.cloned.1.call-update) | async-done | bytes 1048592 | tf_op jit(solution)/shard_map/all_gather | solution.py:93
  131.6 2.3 %fusion = (f32[8,128]{1,0:T(8,128)S(1)}, f32[2048,128,8]{1,0,2:T(8,128)S(1)}) fusion(f32[8]{0:T(128)S(1)} %broadcast_multiply_fusion, pred[128,2048]{0,1:T(8,128)(4,1)S(1)} %broadcast_compare_fusion, bf16[16,8,8,128]{3,2,1,0:T(8,128)(2,1)S(1)} %fusion.8, bf16[2,2048,128]{2,1,0:T(8,128)(2,1)} %all-gather.6.cloned.1.call-done), kind=kOutput, calls=%fused_computation.7 | convolution fusion | flops 543161344 | bytes 9441312 | tf_op jit(solution)/shard_map/qngd,knd->ngqk/dot_general | solution.py:105
  133.9 2.1 %fusion.1 = f32[8,128]{1,0:T(8,128)S(1)} fusion(f32[2048,128,8]{1,0,2:T(8,128)S(1)} %get-tuple-element.10, f32[8,128]{1,0:T(8,128)S(1)} %broadcast_maximum_fusion, f32[8]{0:T(128)S(1)} %broadcast_multiply_fusion, pred[128,2048]{0,1:T(8,128)(4,1)S(1)} %broadcast_compare_fusion), kind=kLoop, calls=%fused_computation.8 | loop fusion | flops 10484736 | bytes 8658976 | tf_op jit(solution)/shard_map/reduce_sum | solution.py:109
  136.0 2.8 %fusion.21 = bf16[8,128,128]{1,2,0:T(8,128)(2,1)} fusion(f32[2048,128,8]{1,0,2:T(8,128)S(1)} %get-tuple-element.10, f32[8,128]{1,0:T(8,128)S(1)} %broadcast_maximum_fusion, f32[8]{0:T(128)S(1)} %broadcast_multiply_fusion, pred[128,2048]{0,1:T(8,128)(4,1)S(1)} %broadcast_compare_fusion, bf16[2,2048,128]{2,1,0:T(8,128)(2,1)S(1)} %copy-done.2, ...), kind=kOutput, calls=%fused_computation.34 | convolution fusion | flops 547618816 | bytes 9445888 | tf_op jit(solution)/shard_map/ngqk,knd->ngqd/dot_general | solution.py:110
  139.5 26.0 %all-gather.8.cloned.1.call-done = bf16[128,8192]{0,1:T(8,128)(2,1)} async-done(((bf16[128,1024]{0,1:T(8,128)(2,1)}), bf16[128,8192]{0,1:T(8,128)(2,1)}) %all-gather.8.cloned.1.call-update) | async-done | bytes 2097168 | tf_op jit(solution)/shard_map/all_gather | solution.py:123
  165.5 5.3 %fusion.10 = bf16[16,8,512]{2,1,0:T(8,128)(2,1)S(1)} fusion(bf16[128,8192]{0,1:T(8,128)(2,1)} %all-gather.8.cloned.1.call-done, bf16[8192,512]{1,0:T(8,128)(2,1)} %param.16, f32[128]{0:T(128)S(1)} %fusion.16), kind=kOutput, calls=%fused_computation.22 | convolution fusion | flops 1073872896 | bytes 10617344 | tf_op jit(solution)/shard_map/dot_general | solution.py:122
  171.5 0.7 copy.42
  172.3 6.5 %all-to-all-start.1 = ((bf16[2,16,8,512]{3,2,0,1:T(8,128)(2,1)}), bf16[2,16,8,512]{3,2,0,1:T(8,128)(2,1)S(1)}, u32[]{:S(2)}, u32[]{:S(2)}) async-start(bf16[2,16,8,512]{3,2,0,1:T(8,128)(2,1)} %copy.42), calls=%async_computation.1 | async-start | bytes 524288 | tf_op jit(solution)/shard_map/all_to_all | solution.py:129
  178.8 1.6 convert_element_type.45
  180.5 6.6 %all-to-all-done.1 = bf16[2,16,8,512]{3,2,0,1:T(8,128)(2,1)S(1)} async-done(((bf16[2,16,8,512]{3,2,0,1:T(8,128)(2,1)}), bf16[2,16,8,512]{3,2,0,1:T(8,128)(2,1)S(1)}, u32[]{:S(2)}, u32[]{:S(2)}) %all-to-all-start.1) | async-done | bytes 262176 | tf_op jit(solution)/shard_map/all_to_all | solution.py:129
  187.3 5.2 %scatter_custom_fusion = f32[1024,512]{1,0:T(8,128)} fusion(f32[1024,512]{1,0:T(8,128)} %convert_element_type.45, s32[256]{0:T(256)S(1)} %bitcast.128, bf16[256,512]{1,0:T(8,128)(2,1)S(1)} %bitcast_select_fusion.1), kind=kCustom, calls=%fused_computation.40 | custom fusion | flops 262144 | bytes 2359296 | tf_op jit(solution)/shard_map/scatter-add | solution.py:133
  192.5 2.7 %convert_element_type.59 = bf16[1024,512]{1,0:T(8,128)(2,1)} convert(f32[1024,512]{1,0:T(8,128)} %scatter_custom_fusion) | non-fusion elementwise | flops 524288 | bytes 3145728 | tf_op jit(solution)/shard_map/convert_element_type | solution.py:135
  (54 shorter events, 6.9 us)
Async XLA Ops:
  6.5 82.9 %copy-start = (bf16[4096,128]{1,0:T(8,128)(2,1)S(1)}, bf16[4096,128]{1,0:T(8,128)(2,1)}, u32[]{:S(2)}) copy-start(bf16[4096,128]{1,0:T(8,128)(2,1)} %param.14) | copy-start | bytes 3145732
  6.5 35.7 %all-gather.4.cloned.1.call-start = ((), (), s32[]{:S(2)}) async-start(), calls=%async_computation.2 | async-start | bytes 2359296 | tf_op jit(solution)/shard_map/all_gather | solution.py:62
  46.1 6.7 %copy-start.3 = (bf16[4096]{0:T(1024)(128)(2,1)S(1)}, bf16[4096]{0:T(1024)(128)(2,1)}, u32[]{:S(2)}) copy-start(bf16[4096]{0:T(1024)(128)(2,1)} %param.11) | copy-start | bytes 24580
  46.1 39.3 %all-to-all-start = ((bf16[2,16,8,4096]{3,2,0,1:T(8,128)(2,1)}), bf16[2,16,8,4096]{3,2,0,1:T(8,128)(2,1)S(1)}, u32[]{:S(2)}, u32[]{:S(2)}) async-start(bf16[2,16,8,4096]{3,2,0,1:T(8,128)(2,1)} %copy.48), calls=%async_computation | async-start | bytes 4194304 | tf_op jit(solution)/shard_map/all_to_all | solution.py:66
  52.8 78.8 %all-gather.6.cloned.1.call-start = ((), (), s32[]{:S(2)}) async-start(), calls=%async_computation.3 | async-start | bytes 1114112 | tf_op jit(solution)/shard_map/all_gather | solution.py:93
  90.0 2.5 %copy-start.5 = (f32[8]{0:T(128)S(1)}, f32[8]{0:T(128)}, u32[]{:S(2)}) copy-start(f32[8]{0:T(128)} %param.17) | copy-start | bytes 100
  92.4 73.1 %all-gather.8.cloned.1.call-start = ((), (), s32[]{:S(2)}) async-start(), calls=%async_computation.4 | async-start | bytes 2359296 | tf_op jit(solution)/shard_map/all_gather | solution.py:123
  133.9 2.1 %copy-start.2 = (bf16[2,2048,128]{2,1,0:T(8,128)(2,1)S(1)}, bf16[2,2048,128]{2,1,0:T(8,128)(2,1)}, u32[]{:S(2)}) copy-start(bf16[2,2048,128]{2,1,0:T(8,128)(2,1)} %all-gather.6.cloned.1.call-done) | copy-start | bytes 3145732
  136.0 2.8 %copy-start.4 = (bf16[4096]{0:T(1024)(128)(2,1)S(1)}, bf16[4096]{0:T(1024)(128)(2,1)}, u32[]{:S(2)}) copy-start(bf16[4096]{0:T(1024)(128)(2,1)} %param.12) | copy-start | bytes 24580
  170.8 8.0 %copy-start.1 = (bf16[1024,512]{1,0:T(8,128)(2,1)S(1)}, bf16[1024,512]{1,0:T(8,128)(2,1)}, u32[]{:S(2)}) copy-start(bf16[1024,512]{1,0:T(8,128)(2,1)} %param.10) | copy-start | bytes 3145732
  172.3 14.8 %all-to-all-start.1 = ((bf16[2,16,8,512]{3,2,0,1:T(8,128)(2,1)}), bf16[2,16,8,512]{3,2,0,1:T(8,128)(2,1)S(1)}, u32[]{:S(2)}, u32[]{:S(2)}) async-start(bf16[2,16,8,512]{3,2,0,1:T(8,128)(2,1)} %copy.42), calls=%async_computation.1 | async-start | bytes 524288 | tf_op jit(solution)/shard_map/all_to_all | solution.py:129
Sparse Core Ops, SparseCore 0:
  13.2 29.0 all-gather.3
  92.5 38.9 all-gather.5
  139.0 26.4 all-gather.7
where the time goes:
time: 202 us
  waiting for transfers between devices  125 us (62%)
  other arithmetic  20.7 us (10%)
  matrix products  17.7 us (9%)
  between operations  15.3 us (8%)
  starting transfers between devices  13.2 us (7%)
  local copies, waits for them, and re-layouts  9.37 us (5%)
    all_gather x1, waiting for transfers between devices, on_device(): piece = lax.all_gather(paired, 'seq', axis=1, tiled=True)  34 us
    all_to_all x1, waiting for transfers between devices, on_device(): lax.all_to_all(outgoing, 'seq', split_axis=1, concat_axis=1, tiled=True)  32.2 us
    all_gather x1, waiting for transfers between devices, on_device(): whole_rows = lax.all_gather(gathered_rows, 'mp', axis=1, tiled=True)  26.6 us
    all_gather x1, waiting for transfers between devices, on_device(): lax.all_gather(attended, 'mp', axis=1, tiled=True)  26 us
    all_to_all x1, starting transfers between devices, on_device(): lax.all_to_all(outgoing, 'seq', split_axis=1, concat_axis=1, tiled=True)  6.64 us
    all_to_all x1, waiting for transfers between devices, on_device(): lax.all_to_all(outgoing_back, 'seq', split_axis=1, concat_axis=1, tiled=T...  6.56 us
    all_to_all x1, starting transfers between devices, on_device(): lax.all_to_all(outgoing_back, 'seq', split_axis=1, concat_axis=1, tiled=T...  6.52 us
    dot_general x1, matrix products, on_device(): jnp.dot(lax.all_gather(attended, 'mp', axis=1, tiled=True), final_project...  5.31 us
  transfers between devices with their start and end apart: 5, of which 5 were waited for; matrix products, arithmetic and copies ran while one was open for 4% of the time, Pallas kernels for 0%

commit v1 on v0

--- a/solution.py
+++ b/solution.py
@@ -126,7 +126,12 @@
     )
     delta = (gate[:, None] * projected).astype(jnp.bfloat16)
     outgoing_back = build_return(delta, prefix, spans, shard, nseq, block_rows)
-    coming_back = lax.all_to_all(outgoing_back, "seq", split_axis=1, concat_axis=1, tiled=True)
+    coming_back = jnp.concatenate(
+        lax.all_to_all(
+            jnp.stack(jnp.split(outgoing_back, lax.axis_size("seq"), axis=1)), "seq", 0, 0
+        ),
+        axis=1,
+    )
     restored = jnp.roll(coming_back, -rotation, axis=1).reshape(slots, delta.shape[1])
     restored = jnp.where(live[:, None], restored, jnp.zeros_like(restored))
     updated = (

time: 202 us -> 211 us (1.045)
  local copies, waits for them, and re-layouts: 9.37 us -> 18.3 us
    unnamed x14 -> x29, local copies, waits for them, and re-layouts: 1.53 us -> 10.6 us
where the time goes in v1:
time: 211 us
  waiting for transfers between devices  125 us (59%)
  other arithmetic  20.7 us (10%)
  local copies, waits for them, and re-layouts  18.3 us (9%)
  matrix products  17.7 us (8%)
  between operations  15.3 us (7%)
  starting transfers between devices  13.2 us (6%)
    all_gather x1, waiting for transfers between devices, on_device(): piece = lax.all_gather(paired, 'seq', axis=1, tiled=True)  34 us
    all_to_all x1, waiting for transfers between devices, on_device(): lax.all_to_all(outgoing, 'seq', split_axis=1, concat_axis=1, tiled=True)  32.2 us
    all_gather x1, waiting for transfers between devices, on_device(): whole_rows = lax.all_gather(gathered_rows, 'mp', axis=1, tiled=True)  26.6 us
    all_gather x1, waiting for transfers between devices, on_device(): lax.all_gather(attended, 'mp', axis=1, tiled=True)  26 us
    unnamed x29, local copies, waits for them, and re-layouts  10.6 us
    all_to_all x1, starting transfers between devices, on_device(): lax.all_to_all(outgoing, 'seq', split_axis=1, concat_axis=1, tiled=True)  6.64 us
    all_to_all x1, waiting for transfers between devices, on_device(): lax.all_to_all(jnp.stack(jnp.split(outgoing_back, lax.axis_size('seq'), a...  6.56 us
    all_to_all x1, starting transfers between devices, on_device(): lax.all_to_all(jnp.stack(jnp.split(outgoing_back, lax.axis_size('seq'), a...  6.52 us
  transfers between devices with their start and end apart: 5, of which 5 were waited for; matrix products, arithmetic and copies ran while one was open for 4% of the time, Pallas kernels for 0%

profile of v1, /device:TPU:1, one launch (start us, length us, event | category | flops | bytes accessed | tf_op | source)
XLA Modules:
  0.0 210.7 jit_solution(2603875998997733254)
XLA Ops:
  6.5 0.9 reduce_sum.69
  9.0 0.7 compare_select_fusion
  9.7 2.6 %gather_fusion = bf16[256,512]{1,0:T(8,128)(2,1)S(1)} fusion(bf16[1024,512]{1,0:T(8,128)(2,1)} %param.10, s32[1024]{0:T(1024)S(1)} %pad_clamp_fusion.2), kind=kCustom, calls=%fused_computation | custom fusion | bytes 525312 | tf_op jit(solution)/shard_map/gather | solution.py:60
  12.3 0.8 broadcast_select_fusion
  15.6 26.6 %all-gather.4.cloned.1.call-done = bf16[256,4096]{1,0:T(8,128)(2,1)} async-done(((bf16[256,512]{1,0:T(8,128)(2,1)}), bf16[256,4096]{1,0:T(8,128)(2,1)}) %all-gather.4.cloned.1.call-update) | async-done | bytes 2097168 | tf_op jit(solution)/shard_map/all_gather | solution.py:62
  42.3 2.4 %fusion.7 = bf16[2,16,8,4096]{3,2,1,0:T(8,128)(2,1)S(1)} fusion(s32[]{:T(128)S(6)} %select_n.208, bf16[2,16,8,4096]{3,2,1,0:T(8,128)(2,1)} %bitcast.221), kind=kLoop, calls=%fused_computation.15 | loop fusion | flops 1048576 | bytes 4194308 | tf_op jit(solution)/shard_map/jit(_roll_dynamic)/concatenate | solution.py:63
  44.6 1.5 copy.108
  46.1 6.6 %all-to-all-start = ((bf16[2,16,8,4096]{3,2,0,1:T(8,128)(2,1)}), bf16[2,16,8,4096]{3,2,0,1:T(8,128)(2,1)S(1)}, u32[]{:S(2)}, u32[]{:S(2)}) async-start(bf16[2,16,8,4096]{3,2,0,1:T(8,128)(2,1)} %copy.108), calls=%async_computation | async-start | bytes 4194304 | tf_op jit(solution)/shard_map/all_to_all | solution.py:66
  53.2 32.2 %all-to-all-done = bf16[2,16,8,4096]{3,2,0,1:T(8,128)(2,1)S(1)} async-done(((bf16[2,16,8,4096]{3,2,0,1:T(8,128)(2,1)}), bf16[2,16,8,4096]{3,2,0,1:T(8,128)(2,1)S(1)}, u32[]{:S(2)}, u32[]{:S(2)}) %all-to-all-start) | async-done | bytes 2097184 | tf_op jit(solution)/shard_map/all_to_all | solution.py:66
  85.4 1.5 copy.84
  86.9 2.2 %gather_fusion.1 = bf16[16,8,4096]{2,1,0:T(8,128)(2,1)S(1)} fusion(bf16[32,8,4096]{2,1,0:T(8,128)(2,1)} %bitcast.220, s32[1024]{0:T(1024)S(1)} %pad_clamp_fusion.1), kind=kCustom, calls=%fused_computation.1 | custom fusion | bytes 2097216 | tf_op jit(solution)/shard_map/gather | solution.py:22
  90.0 1.7 fusion.12
  92.9 4.7 %fusion.8 = bf16[16,8,8,128]{3,2,1,0:T(8,128)(2,1)S(1)} fusion(bf16[4096,1024]{1,0:T(8,128)(2,1)} %param.13, bf16[16,8,4096]{2,1,0:T(8,128)(2,1)S(1)} %gather_fusion.1, f32[4096]{0:T(1024)S(1)} %convert_element_type.49, f32[128]{0:T(128)S(1)} %rsqrt.12), kind=kOutput, calls=%fused_computation.20 | convolution fusion | flops 1075970048 | bytes 9716224 | tf_op jit(solution)/shard_map/dot_general | solution.py:72
  97.6 34.0 %all-gather.6.cloned.1.call-done = bf16[2,2048,128]{2,1,0:T(8,128)(2,1)} async-done(((bf16[2,128,128]{2,1,0:T(8,128)(2,1)}), bf16[2,2048,128]{2,1,0:T(8,128)(2,1)}) %all-gather.6.cloned.1.call-update) | async-done | bytes 1048592 | tf_op jit(solution)/shard_map/all_gather | solution.py:93
  131.6 2.3 %fusion = (f32[8,128]{1,0:T(8,128)S(1)}, f32[2048,128,8]{1,0,2:T(8,128)S(1)}) fusion(f32[8]{0:T(128)S(1)} %broadcast_multiply_fusion, pred[128,2048]{0,1:T(8,128)(4,1)S(1)} %broadcast_compare_fusion, bf16[16,8,8,128]{3,2,1,0:T(8,128)(2,1)S(1)} %fusion.8, bf16[2,2048,128]{2,1,0:T(8,128)(2,1)} %all-gather.6.cloned.1.call-done), kind=kOutput, calls=%fused_computation.7 | convolution fusion | flops 543161344 | bytes 9441312 | tf_op jit(solution)/shard_map/qngd,knd->ngqk/dot_general | solution.py:105
  133.9 2.1 %fusion.1 = f32[8,128]{1,0:T(8,128)S(1)} fusion(f32[2048,128,8]{1,0,2:T(8,128)S(1)} %get-tuple-element.10, f32[8,128]{1,0:T(8,128)S(1)} %broadcast_maximum_fusion, f32[8]{0:T(128)S(1)} %broadcast_multiply_fusion, pred[128,2048]{0,1:T(8,128)(4,1)S(1)} %broadcast_compare_fusion), kind=kLoop, calls=%fused_computation.8 | loop fusion | flops 10484736 | bytes 8658976 | tf_op jit(solution)/shard_map/reduce_sum | solution.py:109
  136.0 2.8 %fusion.21 = bf16[8,128,128]{1,2,0:T(8,128)(2,1)} fusion(f32[2048,128,8]{1,0,2:T(8,128)S(1)} %get-tuple-element.10, f32[8,128]{1,0:T(8,128)S(1)} %broadcast_maximum_fusion, f32[8]{0:T(128)S(1)} %broadcast_multiply_fusion, pred[128,2048]{0,1:T(8,128)(4,1)S(1)} %broadcast_compare_fusion, bf16[2,2048,128]{2,1,0:T(8,128)(2,1)S(1)} %copy-done.2, ...), kind=kOutput, calls=%fused_computation.34 | convolution fusion | flops 547618816 | bytes 9445888 | tf_op jit(solution)/shard_map/ngqk,knd->ngqd/dot_general | solution.py:110
  139.5 26.0 %all-gather.8.cloned.1.call-done = bf16[128,8192]{0,1:T(8,128)(2,1)} async-done(((bf16[128,1024]{0,1:T(8,128)(2,1)}), bf16[128,8192]{0,1:T(8,128)(2,1)}) %all-gather.8.cloned.1.call-update) | async-done | bytes 2097168 | tf_op jit(solution)/shard_map/all_gather | solution.py:123
  165.5 5.3 %fusion.10 = bf16[16,8,512]{2,1,0:T(8,128)(2,1)S(1)} fusion(bf16[128,8192]{0,1:T(8,128)(2,1)} %all-gather.8.cloned.1.call-done, bf16[8192,512]{1,0:T(8,128)(2,1)} %param.16, f32[128]{0:T(128)S(1)} %fusion.16), kind=kOutput, calls=%fused_computation.22 | convolution fusion | flops 1073872896 | bytes 10617344 | tf_op jit(solution)/shard_map/dot_general | solution.py:122
  181.3 6.5 %all-to-all-start.1 = ((bf16[16,2,1,8,512]{4,3,1,2,0:T(8,128)(2,1)}), bf16[16,2,1,8,512]{4,3,1,2,0:T(8,128)(2,1)S(1)}, u32[]{:S(2)}, u32[]{:S(2)}) async-start(bf16[16,2,1,8,512]{4,3,1,2,0:T(8,128)(2,1)} %constant_dynamic-update-slice_fusion), calls=%async_computation.1 | async-start | bytes 524288 | tf_op jit(solution)/shard_map/all_to_all | solution.py:130
  187.8 1.6 convert_element_type.45
  189.5 6.6 %all-to-all-done.1 = bf16[16,2,1,8,512]{4,3,1,2,0:T(8,128)(2,1)S(1)} async-done(((bf16[16,2,1,8,512]{4,3,1,2,0:T(8,128)(2,1)}), bf16[16,2,1,8,512]{4,3,1,2,0:T(8,128)(2,1)S(1)}, u32[]{:S(2)}, u32[]{:S(2)}) %all-to-all-start.1) | async-done | bytes 262176 | tf_op jit(solution)/shard_map/all_to_all | solution.py:130
  196.3 5.2 %scatter_custom_fusion = f32[1024,512]{1,0:T(8,128)} fusion(f32[1024,512]{1,0:T(8,128)} %convert_element_type.45, s32[256]{0:T(256)S(1)} %bitcast.226, bf16[256,512]{1,0:T(8,128)(2,1)S(1)} %bitcast_select_fusion.1), kind=kCustom, calls=%fused_computation.40 | custom fusion | flops 262144 | bytes 2359296 | tf_op jit(solution)/shard_map/scatter-add | solution.py:138
  201.4 2.7 %convert_element_type.59 = bf16[1024,512]{1,0:T(8,128)(2,1)} convert(f32[1024,512]{1,0:T(8,128)} %scatter_custom_fusion) | non-fusion elementwise | flops 524288 | bytes 3145728 | tf_op jit(solution)/shard_map/convert_element_type | solution.py:140
  (69 shorter events, 15.9 us)
Async XLA Ops:
  6.5 82.9 %copy-start = (bf16[4096,128]{1,0:T(8,128)(2,1)S(1)}, bf16[4096,128]{1,0:T(8,128)(2,1)}, u32[]{:S(2)}) copy-start(bf16[4096,128]{1,0:T(8,128)(2,1)} %param.14) | copy-start | bytes 3145732
  6.5 35.7 %all-gather.4.cloned.1.call-start = ((), (), s32[]{:S(2)}) async-start(), calls=%async_computation.2 | async-start | bytes 2359296 | tf_op jit(solution)/shard_map/all_gather | solution.py:62
  46.1 6.7 %copy-start.3 = (bf16[4096]{0:T(1024)(128)(2,1)S(1)}, bf16[4096]{0:T(1024)(128)(2,1)}, u32[]{:S(2)}) copy-start(bf16[4096]{0:T(1024)(128)(2,1)} %param.11) | copy-start | bytes 24580
  46.1 39.3 %all-to-all-start = ((bf16[2,16,8,4096]{3,2,0,1:T(8,128)(2,1)}), bf16[2,16,8,4096]{3,2,0,1:T(8,128)(2,1)S(1)}, u32[]{:S(2)}, u32[]{:S(2)}) async-start(bf16[2,16,8,4096]{3,2,0,1:T(8,128)(2,1)} %copy.108), calls=%async_computation | async-start | bytes 4194304 | tf_op jit(solution)/shard_map/all_to_all | solution.py:66
  52.8 78.8 %all-gather.6.cloned.1.call-start = ((), (), s32[]{:S(2)}) async-start(), calls=%async_computation.3 | async-start | bytes 1114112 | tf_op jit(solution)/shard_map/all_gather | solution.py:93
  90.0 2.5 %copy-start.5 = (f32[8]{0:T(128)S(1)}, f32[8]{0:T(128)}, u32[]{:S(2)}) copy-start(f32[8]{0:T(128)} %param.17) | copy-start | bytes 100
  92.4 73.1 %all-gather.8.cloned.1.call-start = ((), (), s32[]{:S(2)}) async-start(), calls=%async_computation.4 | async-start | bytes 2359296 | tf_op jit(solution)/shard_map/all_gather | solution.py:123
  133.9 2.1 %copy-start.2 = (bf16[2,2048,128]{2,1,0:T(8,128)(2,1)S(1)}, bf16[2,2048,128]{2,1,0:T(8,128)(2,1)}, u32[]{:S(2)}) copy-start(bf16[2,2048,128]{2,1,0:T(8,128)(2,1)} %all-gather.6.cloned.1.call-done) | copy-start | bytes 3145732
  136.0 2.8 %copy-start.4 = (bf16[4096]{0:T(1024)(128)(2,1)S(1)}, bf16[4096]{0:T(1024)(128)(2,1)}, u32[]{:S(2)}) copy-start(bf16[4096]{0:T(1024)(128)(2,1)} %param.12) | copy-start | bytes 24580
  170.8 17.0 %copy-start.1 = (bf16[1024,512]{1,0:T(8,128)(2,1)S(1)}, bf16[1024,512]{1,0:T(8,128)(2,1)}, u32[]{:S(2)}) copy-start(bf16[1024,512]{1,0:T(8,128)(2,1)} %param.10) | copy-start | bytes 3145732
  181.3 14.8 %all-to-all-start.1 = ((bf16[16,2,1,8,512]{4,3,1,2,0:T(8,128)(2,1)}), bf16[16,2,1,8,512]{4,3,1,2,0:T(8,128)(2,1)S(1)}, u32[]{:S(2)}, u32[]{:S(2)}) async-start(bf16[16,2,1,8,512]{4,3,1,2,0:T(8,128)(2,1)} %constant_dynamic-update-slice_fusion), calls=%async_computation.1 | async-start | bytes 524288 | tf_op jit(solution)/shard_map/all_to_all | solution.py:130
Sparse Core Ops, SparseCore 0:
  13.2 29.0 all-gather.3
  92.5 38.9 all-gather.5
  139.0 26.4 all-gather.7
